TPU v7x, 512 devices: a whole 4x8x8 slice. The times are simulated.
512 devices in a mesh: lat: 8 (over z_lo, core), lon: 64 (over z_hi, x, y).
Axes of the slice: x: 4, y: 8, z: 8 (z_hi: 2, z_lo: 4; z = z_hi * 4 + z_lo), core: 2. Of those that a mesh axis runs over, the one named last changes fastest.
Arguments:
- background_state: bfloat16 [18, 5760, 1024], P(None, 'lon', 'lat'), may hold values from -6 to 6
- perturbation: bfloat16 [18, 5760, 1024], P(None, 'lon', 'lat'), may hold values from -16 to 16
- surface_pattern_index: int32 [5760, 1024], P('lon', 'lat'), may hold values from 0 to 15
- surface_amplitude_table: float32 [16], replicated, may hold values from -4 to 4
- cutoff: int32 [1024], P('lat'), may hold values from 4 to 64, as said below
- zonal_row_weight: float32 [1024], P('lat'), may hold values from 0.5 to 2
- diffusivity: float32 [18], replicated, may hold values from 0.04 to 0.25
- input_weight: bfloat16 [48, 18], replicated, may hold values from -1.5 to 1.5
- bias: float32 [48], replicated, may hold values from -4 to 4
- output_weight: float32 [18, 48], replicated, may hold values from -0.875 to 0.875
Outputs:
- tangent: bfloat16 [18, 5760, 1024], P(None, 'lon', 'lat')
- gradient: bfloat16 [18, 5760, 1024], P(None, 'lon', 'lat')
Inputs may be any that keep to these rules, and one draw needn't show every extreme that they name: Rows 64 or more rows away from both ends of the grid have cutoff 64; the first and last rows have cutoff 4; a row d < 64 rows from the nearer end has cutoff at least 4 + (d * 60) // 64.
All inputs are finite; a program needn't handle non-finite values.
Results may differ from a plain program's by a relative error of at most 0.001.
Values sent between devices are 32-bit elements; how exact they have to be, the bound alone decides.
A program may use at most 64 MiB of HBM per device.

v0:
```python
import math
import jax
import jax.numpy as jnp
from jax import lax
from jax.sharding import PartitionSpec as P

LONGITUDE_COUNT = 5760
KW = 64
POLAR = 64
TOP_PRECISION = lax.Precision.HIGHEST


def padded(x, sides, width, wrap):
    for axis, dim in sides:
        count, length = (lax.axis_size(axis), x.shape[dim])
        up = [(i, (i + 1) % count) for i in range(count if wrap else count - 1)]
        down = [(j, i) for i, j in up]
        last = lax.slice_in_dim(x, length - width, length, axis=dim)
        leading = lax.slice_in_dim(x, 0, width, axis=dim)
        before = lax.ppermute(last, axis, up)
        after = lax.ppermute(leading, axis, down)
        x = jnp.concatenate([before, x, after], axis=dim)
    return x


def spectral_table(longitudes):
    wave_numbers = jnp.arange(1, KW + 1, dtype=jnp.int32)
    phase_index = longitudes[:, None] * wave_numbers[None, :] % LONGITUDE_COUNT
    angles = phase_index.astype(jnp.float32) * (2.0 * math.pi / LONGITUDE_COUNT)
    return jnp.concatenate([jnp.cos(angles), jnp.sin(angles)], axis=1)


def removal_weights(cutoff):
    wave_numbers = jnp.arange(1, KW + 1, dtype=jnp.float32)[:, None]
    cut_limit = cutoff.astype(jnp.float32)[None, :]
    cut_ratio = cut_limit / wave_numbers
    damping = jnp.where(wave_numbers > cut_limit, 1.0 - cut_ratio * cut_ratio, 0.0)
    return jnp.concatenate([damping, damping], axis=0)


def analyze(state_grid_field, fourier_basis_table):
    return jnp.einsum("hpu,pa->hau", state_grid_field, fourier_basis_table, precision=TOP_PRECISION)


def rebuild(fourier_spectra, fourier_basis_table):
    return jnp.einsum(
        "zum,gu->zgm", fourier_spectra, fourier_basis_table, precision=TOP_PRECISION
    ) * (2.0 / LONGITUDE_COUNT)


def diffuse(state_grid_field, diffusivity, zonal_row_weight):
    cycle_padded = padded(state_grid_field, (("lon", 1),), 1, True)
    band_padded = padded(state_grid_field, (("lat", 2),), 1, False)
    zonal_term = cycle_padded[:, 2:, :] + cycle_padded[:, :-2, :] - 2.0 * state_grid_field
    meridional = band_padded[:, :, 2:] + band_padded[:, :, :-2] - 2.0 * state_grid_field
    return diffusivity[:, None, None] * (zonal_row_weight[None, None, :] * zonal_term + meridional)


def summed_spectra(polar_slab, fourier_basis_table):
    local_spectra = analyze(polar_slab, fourier_basis_table)
    return lax.psum(local_spectra, "lon")


def cycle_filter(polar_slab, weight_set, fourier_basis_table):
    fourier_spectra = summed_spectra(polar_slab, fourier_basis_table)
    filtered = polar_slab - rebuild(fourier_spectra * weight_set[None], fourier_basis_table)
    return (filtered,)


def per_device(
    background_state,
    perturbation,
    surface_pattern_index,
    surface_amplitude_table,
    cutoff,
    zonal_row_weight,
    diffusivity,
    input_weight,
    bias,
    output_weight,
):
    lon_dev = background_state.shape[1]
    lat_dev = background_state.shape[2]
    pattern_values = jnp.arange(surface_amplitude_table.shape[0], dtype=jnp.int32)
    surface_field = jnp.sum(
        jnp.where(
            surface_pattern_index[None] == pattern_values[:, None, None],
            surface_amplitude_table[:, None, None],
            0.0,
        ),
        axis=0,
    )
    start_pert = perturbation.astype(jnp.float32)
    perturbation_field = jnp.concatenate(
        [start_pert[:1] + surface_field[None], start_pert[1:]], axis=0
    )
    before_activation = (
        jnp.einsum(
            "vb,bqf->vqf", input_weight, background_state, preferred_element_type=jnp.float32
        )
        + bias[:, None, None]
    )
    active = jnp.tanh(before_activation)
    activation_slope = 1.0 - active * active
    wide_weight = input_weight.astype(jnp.float32)
    hidden_forward = (
        jnp.einsum("vb,bqf->vqf", wide_weight, perturbation_field, precision=TOP_PRECISION)
        * activation_slope
    )
    tangent_image = (
        perturbation_field
        + diffuse(perturbation_field, diffusivity, zonal_row_weight)
        + 0.5 * jnp.einsum("sm,mxq->sxq", output_weight, hidden_forward, precision=TOP_PRECISION)
    )
    last_band = lax.axis_index("lat") == lax.axis_size("lat") - 1

    def orient(values_in):
        return jnp.where(last_band, jnp.flip(values_in, axis=-1), values_in)

    slab_start = jnp.where(last_band, lat_dev - POLAR, 0).astype(jnp.int32)
    polar_cut = orient(lax.dynamic_slice_in_dim(cutoff, slab_start, POLAR, 0))
    weight_set = removal_weights(polar_cut)
    longitudes = lax.axis_index("lon") * lon_dev + jnp.arange(lon_dev, dtype=jnp.int32)
    fourier_basis_table = spectral_table(longitudes)

    def spectral(polar_slab):
        return cycle_filter(polar_slab, weight_set, fourier_basis_table)

    polar_slab = orient(lax.dynamic_slice_in_dim(tangent_image, slab_start, POLAR, 2))
    filtered = spectral(polar_slab)[0]
    tangent_full = lax.dynamic_update_slice_in_dim(tangent_image, orient(filtered), slab_start, 2)
    twice = spectral(orient(lax.dynamic_slice_in_dim(tangent_full, slab_start, POLAR, 2)))[0]
    adjoint_input = lax.dynamic_update_slice_in_dim(tangent_full, orient(twice), slab_start, 2)
    hidden_backward = (
        jnp.einsum("xf,xbe->fbe", output_weight, adjoint_input, precision=TOP_PRECISION)
        * activation_slope
    )
    gradient = (
        adjoint_input
        + diffuse(adjoint_input, diffusivity, zonal_row_weight)
        + 0.5 * jnp.einsum("zo,zmf->omf", wide_weight, hidden_backward, precision=TOP_PRECISION)
    )
    return (tangent_full.astype(jnp.bfloat16), gradient.astype(jnp.bfloat16))


def solution(mesh):
    placed = (
        P(None, "lon", "lat"),
        P(None, "lon", "lat"),
        P("lon", "lat"),
        P(),
        P("lat"),
        P("lat"),
        P(),
        P(),
        P(),
        P(),
    )
    return jax.shard_map(
        per_device,
        mesh=mesh,
        in_specs=placed,
        out_specs=(P(None, "lon", "lat"), P(None, "lon", "lat")),
        check_vma=False,
    )
```

profile of v0, /device:TPU:1, one launch (start us, length us, event | category | flops | bytes accessed | tf_op | source)
XLA Modules:
  0.0 1695.8 jit_solution(2790603785789324412)
XLA Ops:
  7.2 1.4 copy.57
  8.6 1.2 convert_element_type.16
  9.9 0.7 copy-done.4
  10.6 0.3 select_reduce_fusion
  11.0 0.9 slice_add_fusion
  11.9 1.5 fusion.2
  13.4 1.6 copy.59
  15.0 16.6 collective-permute-start
  31.6 0.4 copy.61
  31.9 1.9 collective-permute-start.1
  33.9 2.9 collective-permute-start.2
  36.8 3.0 collective-permute-start.3
  39.9 1.5 copy.63
  41.4 3.7 fusion.45
  45.1 1.9 fusion.27
  47.3 4.0 fusion.1
  51.4 1.5 copy.65
  52.9 1.4 copy.60
  54.3 1.4 copy.62
  55.8 3.2 fusion.19
  59.1 0.4 rev.17
  59.6 1.4 fusion.52
  61.7 762.4 %all-reduce.3.cloned.1.call-done = f32[18,128,64]{1,2,0:T(8,128)} async-done(((f32[18,128,64]{1,2,0:T(8,128)}), f32[18,128,64]{1,2,0:T(8,128)}) %all-reduce.3.cloned.1.call-update) | async-done | bytes 589840 | tf_op jit(solution)/shard_map/psum | solution.py:61
  824.2 1.1 broadcast_multiply_fusion.1
  825.3 0.6 fusion.53
  826.0 0.4 rev.19
  826.5 0.4 rev.20
  827.0 1.4 fusion.54
  828.6 1.1 copy.72
  829.7 789.7 %all-reduce.5.cloned.1.call-done = f32[18,128,64]{1,2,0:T(8,128)} async-done(((f32[18,128,64]{1,2,0:T(8,128)}), f32[18,128,64]{1,2,0:T(8,128)}) %all-reduce.5.cloned.1.call-update) | async-done | bytes 589840 | tf_op jit(solution)/shard_map/psum | solution.py:61
  1619.3 1.1 broadcast_multiply_fusion
  1620.4 0.6 fusion.55
  1621.2 0.4 rev.21
  1621.7 1.5 copy.70
  1623.2 1.5 fusion.50
  1624.7 3.3 fusion.38
  1628.0 1.6 copy.66
  1629.6 9.5 collective-permute-start.4
  1639.1 0.4 copy.68
  1639.5 1.9 collective-permute-start.5
  1641.4 32.0 %collective-permute-start.6 = (f32[18,90,1]{1,2,0:T(1,128)S(1)}, f32[18,90,1]{1,2,0:T(1,128)S(1)}, u32[]{:S(2)}, u32[]{:S(2)}) collective-permute-start(f32[18,90,1]{1,2,0:T(1,128)S(1)} %get-tuple-element.14), channel_id=1, source_target_pairs={{64,0},{128,64},{192,128},{256,192},{320,256},{384,320},{448,384},... | collective-permute-start | bytes 19448 | tf_op jit(solution)/shard_map/ppermute | solution.py:21
  1673.4 2.3 collective-permute-start.7
  1675.7 4.6 fusion
  1680.3 1.6 copy.71
  1682.0 1.4 copy.67
  1683.4 1.5 copy.69
  1684.8 3.0 fusion.10
  1687.9 1.1 copy.73
  (55 shorter events, 2.1 us)
Async XLA Ops:
  7.2 37.9 %copy-start = (bf16[18,90,128]{2,1,0:T(8,128)(2,1)S(1)}, bf16[18,90,128]{2,1,0:T(8,128)(2,1)}, u32[]{:S(2)}) copy-start(bf16[18,90,128]{2,1,0:T(8,128)(2,1)} %param.10) | copy-start | bytes 1244164
  7.2 817.0 %all-reduce.3.cloned.1.call-start = ((), (), s32[]{:S(2)}) async-start(), calls=%async_computation | async-start | bytes 1179648 | tf_op jit(solution)/shard_map/psum | solution.py:61
  9.8 0.8 copy-start.4
  9.8 0.8 copy-start.8
  15.0 37.9 %collective-permute-start = (f32[18,1,128]{2,1,0:T(1,128)S(1)}, f32[18,1,128]{2,1,0:T(1,128)S(1)}, u32[]{:S(2)}, u32[]{:S(2)}) collective-permute-start(f32[18,1,128]{2,1,0:T(1,128)S(1)} %copy.59), channel_id=1, source_target_pairs={{1,0},{2,1},{3,2},{4,3},{5,4},{6,5},{7,6},{8,7},{9,8},{10,9},{11,1... | collective-permute-start | bytes 27656 | tf_op jit(solution)/shard_map/ppermute | solution.py:21
  31.9 22.4 %collective-permute-start.1 = (f32[18,1,128]{2,1,0:T(1,128)S(1)}, f32[18,1,128]{2,1,0:T(1,128)S(1)}, u32[]{:S(2)}, u32[]{:S(2)}) collective-permute-start(f32[18,1,128]{2,1,0:T(1,128)S(1)} %copy.61), channel_id=1, source_target_pairs={{0,1},{1,2},{2,3},{3,4},{4,5},{5,6},{6,7},{7,8},{8,9},{9,10},{10,1... | collective-permute-start | bytes 27656 | tf_op jit(solution)/shard_map/ppermute | solution.py:20
  33.9 21.9 %collective-permute-start.2 = (f32[18,90,1]{1,2,0:T(1,128)S(1)}, f32[18,90,1]{1,2,0:T(1,128)S(1)}, u32[]{:S(2)}, u32[]{:S(2)}) collective-permute-start(f32[18,90,1]{1,2,0:T(1,128)S(1)} %get-tuple-element.18), channel_id=1, source_target_pairs={{64,0},{128,64},{192,128},{256,192},{320,256},{384,320},{448,384},... | collective-permute-start | bytes 19448 | tf_op jit(solution)/shard_map/ppermute | solution.py:21
  36.8 19.0 %collective-permute-start.3 = (f32[18,90,1]{1,2,0:T(1,128)S(1)}, f32[18,90,1]{1,2,0:T(1,128)S(1)}, u32[]{:S(2)}, u32[]{:S(2)}) collective-permute-start(f32[18,90,1]{1,2,0:T(1,128)S(1)} %get-tuple-element.19), channel_id=1, source_target_pairs={{0,64},{64,128},{128,192},{192,256},{256,320},{320,384},{384,448},... | collective-permute-start | bytes 19448 | tf_op jit(solution)/shard_map/ppermute | solution.py:20
  39.9 1.5 copy-start.2
  45.1 2.2 copy-start.3
  45.1 2.2 copy-start.5
  52.9 2.9 copy-start.6
  52.9 2.9 copy-start.7
  59.6 1.7 copy-start.9
  61.1 1558.3 %all-reduce.5.cloned.1.call-start = ((), (), s32[]{:S(2)}) async-start(), calls=%async_computation.1 | async-start | bytes 1179648 | tf_op jit(solution)/shard_map/psum | solution.py:61
  1623.2 1.5 copy-start.1
  1629.6 52.4 %collective-permute-start.4 = (f32[18,1,128]{2,1,0:T(1,128)S(1)}, f32[18,1,128]{2,1,0:T(1,128)S(1)}, u32[]{:S(2)}, u32[]{:S(2)}) collective-permute-start(f32[18,1,128]{2,1,0:T(1,128)S(1)} %copy.66), channel_id=1, source_target_pairs={{1,0},{2,1},{3,2},{4,3},{5,4},{6,5},{7,6},{8,7},{9,8},{10,9},{11,1... | collective-permute-start | bytes 27656 | tf_op jit(solution)/shard_map/ppermute | solution.py:21
  1639.5 43.9 %collective-permute-start.5 = (f32[18,1,128]{2,1,0:T(1,128)S(1)}, f32[18,1,128]{2,1,0:T(1,128)S(1)}, u32[]{:S(2)}, u32[]{:S(2)}) collective-permute-start(f32[18,1,128]{2,1,0:T(1,128)S(1)} %copy.68), channel_id=1, source_target_pairs={{0,1},{1,2},{2,3},{3,4},{4,5},{5,6},{6,7},{7,8},{8,9},{9,10},{10,1... | collective-permute-start | bytes 27656 | tf_op jit(solution)/shard_map/ppermute | solution.py:20
  1641.4 43.4 %collective-permute-start.6 = (f32[18,90,1]{1,2,0:T(1,128)S(1)}, f32[18,90,1]{1,2,0:T(1,128)S(1)}, u32[]{:S(2)}, u32[]{:S(2)}) collective-permute-start(f32[18,90,1]{1,2,0:T(1,128)S(1)} %get-tuple-element.14), channel_id=1, source_target_pairs={{64,0},{128,64},{192,128},{256,192},{320,256},{384,320},{448,384},... | collective-permute-start | bytes 19448 | tf_op jit(solution)/shard_map/ppermute | solution.py:21
  1673.4 11.4 collective-permute-start.7
Sparse Core Ops, SparseCore 0:
  61.2 762.9 all-reduce.2
  828.6 790.6 all-reduce.4
where the time goes:
time: 1700 us
  waiting for transfers between devices  1550 us (91%)
  starting transfers between devices  70.3 us (4%)
  local copies, waits for them, and re-layouts  23.7 us (1%)
  matrix products  21.6 us (1%)
    psum x2, waiting for transfers between devices, summed_spectra(): return lax.psum(local_spectra, 'lon')  1550 us
    ppermute x4, starting transfers between devices, padded(): after = lax.ppermute(leading, axis, down)  61 us
  transfers between devices with their start and end apart: 10, of which 2 were waited for; matrix products, arithmetic and copies ran while one was open for 2% of the time, Pallas kernels for 0%

commit v1 on v0

--- a/solution.py
+++ b/solution.py
@@ -58,7 +58,7 @@
 
 def summed_spectra(polar_slab, fourier_basis_table):
     local_spectra = analyze(polar_slab, fourier_basis_table)
-    return lax.psum(local_spectra, "lon")
+    return jnp.sum(lax.all_gather(local_spectra, "lon"), axis=0)
 
 
 def cycle_filter(polar_slab, weight_set, fourier_basis_table):

time: 1700 us -> 1250 us (0.74)
  waiting for transfers between devices: 1550 us -> 1110 us
  starting transfers between devices: 70.3 us -> 43.3 us
  other arithmetic: 13.6 us -> 37.9 us
    psum x2 -> x0, waiting for transfers between devices: 1550 us -> none  [summed_spectra(): return lax.psum(local_spectra, 'lon')]
    all_gather x0 -> x2, waiting for transfers between devices: none -> 1110 us  [summed_spectra(): return jnp.sum(lax.all_gather(local_spectra, 'lon'), axis=0)]
    reduce_sum x0 -> x2, other arithmetic: none -> 26.4 us  [summed_spectra(): return jnp.sum(lax.all_gather(local_spectra, 'lon'), axis=0)]
    ppermute x4, starting transfers between devices: 61 us -> 34.8 us  [padded(): after = lax.ppermute(leading, axis, down)]
where the time goes in v1:
time: 1250 us
  waiting for transfers between devices  1110 us (89%)
  starting transfers between devices  43.3 us (3%)
  other arithmetic  37.9 us (3%)
  local copies, waits for them, and re-layouts  23.1 us (2%)
  matrix products  16.5 us (1%)
  between operations  14.5 us (1%)
    all_gather x2, waiting for transfers between devices, summed_spectra(): return jnp.sum(lax.all_gather(local_spectra, 'lon'), axis=0)  1110 us
    ppermute x4, starting transfers between devices, padded(): after = lax.ppermute(leading, axis, down)  34.8 us
    reduce_sum x2, other arithmetic, summed_spectra(): return jnp.sum(lax.all_gather(local_spectra, 'lon'), axis=0)  26.4 us
  transfers between devices with their start and end apart: 10, of which 2 were waited for; matrix products, arithmetic and copies ran while one was open for 2% of the time, Pallas kernels for 0%

profile of v1, /device:TPU:1, one launch (start us, length us, event | category | flops | bytes accessed | tf_op | source)
XLA Modules:
  0.0 1246.5 jit_solution(17627779570735654853)
XLA Ops:
  7.2 1.4 copy.61
  8.8 1.2 convert_element_type.16
  9.9 0.3 select_reduce_fusion
  10.4 0.9 slice_add_fusion
  11.3 8.8 collective-permute-start.2
  20.0 1.9 collective-permute-start.3
  22.0 1.5 fusion.2
  23.4 1.6 copy.65
  25.1 1.9 collective-permute-start.1
  27.0 0.4 copy.63
  27.4 11.5 collective-permute-start
  39.0 1.5 copy.67
  40.5 2.3 fusion.45
  42.9 0.5 fusion.27
  43.4 0.3 fusion.34
  43.7 1.7 fusion.1
  45.5 1.5 copy.69
  47.0 1.4 copy.64
  48.5 1.4 copy.66
  49.9 3.2 fusion.19
  53.2 0.4 rev.17
  53.8 1.4 fusion.52
  55.9 555.0 %all-gather.5.cloned.1.call-done = f32[1152,128,64]{1,2,0:T(8,128)} async-done(((f32[18,128,64]{1,2,0:T(8,128)}), f32[1152,128,64]{1,2,0:T(8,128)}) %all-gather.5.cloned.1.call-update) | async-done | bytes 37748752 | tf_op jit(solution)/shard_map/all_gather | solution.py:61
  610.9 13.2 %reduce_sum.28 = f32[18,128,64]{1,2,0:T(8,128)S(1)} reduce(f32[64,18,128,64]{2,3,1,0:T(8,128)} %bitcast.60, f32[]{:T(128)} %constant.15.clone.1), dimensions={0}, to_apply=%region_1.2 | reduce | flops 9289728 | bytes 38338564 | tf_op jit(solution)/shard_map/reduce_sum | solution.py:61
  624.2 0.6 fusion.53
  624.9 0.4 rev.19
  625.5 0.4 rev.20
  626.0 1.4 fusion.54
  627.6 1.1 copy.76
  628.6 556.0 %all-gather.7.cloned.1.call-done = f32[1152,128,64]{1,2,0:T(8,128)} async-done(((f32[18,128,64]{1,2,0:T(8,128)}), f32[1152,128,64]{1,2,0:T(8,128)}) %all-gather.7.cloned.1.call-update) | async-done | bytes 37748752 | tf_op jit(solution)/shard_map/all_gather | solution.py:61
  1184.6 13.2 %reduce_sum.29 = f32[18,128,64]{1,2,0:T(8,128)S(1)} reduce(f32[64,18,128,64]{2,3,1,0:T(8,128)} %bitcast.61, f32[]{:T(128)} %constant.15.clone.1), dimensions={0}, to_apply=%region_2.3 | reduce | flops 9289728 | bytes 38338564 | tf_op jit(solution)/shard_map/reduce_sum | solution.py:61
  1197.9 0.6 fusion.55
  1198.6 0.4 rev.21
  1199.1 1.5 copy.74
  1200.7 1.4 fusion.50
  1202.1 3.0 collective-permute-start.6
  1205.1 2.6 collective-permute-start.7
  1207.7 3.3 fusion.38
  1211.0 1.6 copy.70
  1212.6 0.4 copy.72
  1213.0 1.9 collective-permute-start.5
  1214.9 11.5 collective-permute-start.4
  1226.4 4.6 fusion
  1231.0 1.6 copy.75
  1232.7 1.4 copy.71
  1234.1 1.4 copy.73
  1235.6 3.1 fusion.10
  1238.6 1.1 copy.77
  (61 shorter events, 1.9 us)
Async XLA Ops:
  7.2 35.7 %copy-start = (bf16[18,90,128]{2,1,0:T(8,128)(2,1)S(1)}, bf16[18,90,128]{2,1,0:T(8,128)(2,1)}, u32[]{:S(2)}) copy-start(bf16[18,90,128]{2,1,0:T(8,128)(2,1)} %param.10) | copy-start | bytes 1244164
  7.2 603.7 %all-gather.5.cloned.1.call-start = ((), (), s32[]{:S(2)}) async-start(), calls=%async_computation | async-start | bytes 38338560 | tf_op jit(solution)/shard_map/all_gather | solution.py:61
  8.7 1.2 copy-start.6
  8.7 1.2 copy-start.10
  11.3 38.7 %collective-permute-start.2 = (f32[18,90,1]{1,2,0:T(1,128)S(1)}, f32[18,90,1]{1,2,0:T(1,128)S(1)}, u32[]{:S(2)}, u32[]{:S(2)}) collective-permute-start(f32[18,90,1]{1,2,0:T(1,128)S(1)} %get-tuple-element.18), channel_id=1, source_target_pairs={{64,0},{128,64},{192,128},{256,192},{320,256},{384,320},{448,384},... | collective-permute-start | bytes 19448 | tf_op jit(solution)/shard_map/ppermute | solution.py:21
  20.0 29.9 %collective-permute-start.3 = (f32[18,90,1]{1,2,0:T(1,128)S(1)}, f32[18,90,1]{1,2,0:T(1,128)S(1)}, u32[]{:S(2)}, u32[]{:S(2)}) collective-permute-start(f32[18,90,1]{1,2,0:T(1,128)S(1)} %get-tuple-element.19), channel_id=1, source_target_pairs={{0,64},{64,128},{128,192},{192,256},{256,320},{320,384},{384,448},... | collective-permute-start | bytes 19448 | tf_op jit(solution)/shard_map/ppermute | solution.py:20
  25.1 23.4 %collective-permute-start.1 = (f32[18,1,128]{2,1,0:T(1,128)S(1)}, f32[18,1,128]{2,1,0:T(1,128)S(1)}, u32[]{:S(2)}, u32[]{:S(2)}) collective-permute-start(f32[18,1,128]{2,1,0:T(1,128)S(1)} %copy.65), channel_id=1, source_target_pairs={{0,1},{1,2},{2,3},{3,4},{4,5},{5,6},{6,7},{7,8},{8,9},{9,10},{10,1... | collective-permute-start | bytes 27656 | tf_op jit(solution)/shard_map/ppermute | solution.py:20
  27.4 19.7 %collective-permute-start = (f32[18,1,128]{2,1,0:T(1,128)S(1)}, f32[18,1,128]{2,1,0:T(1,128)S(1)}, u32[]{:S(2)}, u32[]{:S(2)}) collective-permute-start(f32[18,1,128]{2,1,0:T(1,128)S(1)} %copy.63), channel_id=1, source_target_pairs={{1,0},{2,1},{3,2},{4,3},{5,4},{6,5},{7,6},{8,7},{9,8},{10,9},{11,1... | collective-permute-start | bytes 27656 | tf_op jit(solution)/shard_map/ppermute | solution.py:21
  39.0 1.6 copy-start.4
  42.9 0.8 copy-start.5
  42.9 0.8 copy-start.7
  43.4 2.0 copy-start.2
  47.0 2.9 copy-start.8
  47.0 2.9 copy-start.9
  53.7 1.7 copy-start.11
  55.2 1129.4 %all-gather.7.cloned.1.call-start = ((), (), s32[]{:S(2)}) async-start(), calls=%async_computation.1 | async-start | bytes 38338560 | tf_op jit(solution)/shard_map/all_gather | solution.py:61
  1200.7 7.0 copy-start.3
  1202.1 33.4 %collective-permute-start.6 = (f32[18,90,1]{1,2,0:T(1,128)S(1)}, f32[18,90,1]{1,2,0:T(1,128)S(1)}, u32[]{:S(2)}, u32[]{:S(2)}) collective-permute-start(f32[18,90,1]{1,2,0:T(1,128)S(1)} %get-tuple-element.14), channel_id=1, source_target_pairs={{64,0},{128,64},{192,128},{256,192},{320,256},{384,320},{448,384},... | collective-permute-start | bytes 19448 | tf_op jit(solution)/shard_map/ppermute | solution.py:21
  1205.1 30.4 %collective-permute-start.7 = (f32[18,90,1]{1,2,0:T(1,128)S(1)}, f32[18,90,1]{1,2,0:T(1,128)S(1)}, u32[]{:S(2)}, u32[]{:S(2)}) collective-permute-start(f32[18,90,1]{1,2,0:T(1,128)S(1)} %get-tuple-element.15), channel_id=1, source_target_pairs={{0,64},{64,128},{128,192},{192,256},{256,320},{320,384},{384,448},... | collective-permute-start | bytes 19448 | tf_op jit(solution)/shard_map/ppermute | solution.py:20
  1213.0 21.1 %collective-permute-start.5 = (f32[18,1,128]{2,1,0:T(1,128)S(1)}, f32[18,1,128]{2,1,0:T(1,128)S(1)}, u32[]{:S(2)}, u32[]{:S(2)}) collective-permute-start(f32[18,1,128]{2,1,0:T(1,128)S(1)} %copy.72), channel_id=1, source_target_pairs={{0,1},{1,2},{2,3},{3,4},{4,5},{5,6},{6,7},{7,8},{8,9},{9,10},{10,1... | collective-permute-start | bytes 27656 | tf_op jit(solution)/shard_map/ppermute | solution.py:20
  1214.9 17.7 %collective-permute-start.4 = (f32[18,1,128]{2,1,0:T(1,128)S(1)}, f32[18,1,128]{2,1,0:T(1,128)S(1)}, u32[]{:S(2)}, u32[]{:S(2)}) collective-permute-start(f32[18,1,128]{2,1,0:T(1,128)S(1)} %copy.70), channel_id=1, source_target_pairs={{1,0},{2,1},{3,2},{4,3},{5,4},{6,5},{7,6},{8,7},{9,8},{10,9},{11,1... | collective-permute-start | bytes 27656 | tf_op jit(solution)/shard_map/ppermute | solution.py:21
  1235.6 4.1 copy-start.1
Sparse Core Ops, SparseCore 0:
  55.3 555.5 all-gather.4
  627.6 557.0 all-gather.6
